TPU v7x, 32 devices: a whole 2x2x4 slice. The times are simulated.
32 devices in a mesh: pb: 4 (over y, x), ka: 8 (over z, core).
Axes of the slice: x: 2, y: 2, z: 4, core: 2. Of those that a mesh axis runs over, the one named last changes fastest.
Arguments:
- feat_first: bfloat16 [8192, 128], P(('pb', 'ka')), may hold values from -16 to 16
- feat_second: bfloat16 [8192, 128], P(('ka', 'pb')), may hold values from -18 to 18
- value_weight: bfloat16 [128, 128], replicated, may hold values from -0.5 to 0.5
- out_weight: bfloat16 [128, 128], replicated, may hold values from -0.5 to 0.5
- conv_weight: bfloat16 [3, 3, 128, 128], replicated, may hold values from -0.1875 to 0.1875
- conv_bias: bfloat16 [128], replicated, may hold values from -3 to 3
Outputs:
- refined: bfloat16 [32, 256, 128], P(('pb', 'ka'))
All inputs are finite; a program needn't handle non-finite values.
Results may differ from a plain program's by a relative error of at most 0.0055.
Values may be sent and summed in bfloat16 or wider, within the bound.
A program may use at most 192 MiB of HBM per device.

v0:
```python
import jax
import jax.numpy as jnp
from jax import lax
from jax.sharding import PartitionSpec as P

WIMG = 256


floor_score = -1e30


def padded_2(block, sides, width):
    for axis, dim in sides:
        count = lax.axis_size(axis)
        forward = [(i, i + 1) for i in range(count - 1)]
        backward = [(target, source) for source, target in forward]
        low = lax.ppermute(
            lax.slice_in_dim(block, block.shape[dim] - width, None, axis=dim), axis, forward
        )
        high = lax.ppermute(lax.slice_in_dim(block, 0, width, axis=dim), axis, backward)
        block = jnp.concatenate([low, block, high], axis=dim)
    return block


def refine(padded, center, conv_weight, conv_bias):
    num_rows, num_cols, channels = center.shape
    accum_sum = jnp.zeros((num_rows * num_cols, channels), jnp.float32)
    for row_shift in range(3):
        for col_shift in range(3):
            window = padded[
                row_shift : row_shift + num_rows, col_shift : col_shift + num_cols
            ].reshape(num_rows * num_cols, channels)
            accum_sum = accum_sum + jnp.dot(
                window, conv_weight[row_shift, col_shift], preferred_element_type=jnp.float32
            )
    conv_out = accum_sum.reshape(num_rows, num_cols, channels) + conv_bias.astype(jnp.float32)
    return (center.astype(jnp.float32) + jax.nn.gelu(conv_out)).astype(jnp.bfloat16)


def local(feat_first, feat_second, value_weight, out_weight, conv_weight, conv_bias):
    own_rows, feat_width = feat_first.shape
    score_scale = feat_width ** (-0.5)
    values = jnp.dot(feat_second, value_weight, preferred_element_type=jnp.float32).astype(
        jnp.bfloat16
    )
    queries = lax.all_gather(feat_first, "ka", axis=0, tiled=True)
    total_rows = queries.shape[0]
    block_rows = min(1024, total_rows)
    num_blocks = total_rows // block_rows
    query_blocks = queries.reshape(num_blocks, block_rows, feat_width)
    start_carry = (
        jnp.full((num_blocks, block_rows), floor_score, jnp.float32),
        jnp.zeros((num_blocks, block_rows), jnp.float32),
        jnp.zeros((num_blocks, block_rows, feat_width), jnp.float32),
    )
    keys_part = lax.all_gather(feat_second, "pb", axis=0, tiled=True)
    values_part = lax.all_gather(values, "pb", axis=0, tiled=True)

    def update(members):
        query_block, old_peak, old_mass, old_weighted = members
        scores = (
            jnp.einsum("qc,kc->qk", query_block, keys_part, preferred_element_type=jnp.float32)
            * score_scale
        )
        new_peak = jnp.maximum(old_peak, jnp.max(scores, axis=1))
        expo = jnp.exp(scores - new_peak[:, None])
        decay_factor = jnp.exp(old_peak - new_peak)
        new_mass = old_mass * decay_factor + jnp.sum(expo, axis=1)
        new_weighted = old_weighted * decay_factor[:, None] + jnp.dot(
            expo.astype(jnp.bfloat16), values_part, preferred_element_type=jnp.float32
        )
        return (new_peak, new_mass, new_weighted)

    row_peak, row_mass, weighted = lax.map(update, (query_blocks,) + tuple(start_carry))
    row_peak = row_peak.reshape(total_rows)
    row_mass = row_mass.reshape(total_rows)
    weighted = weighted.reshape(total_rows, feat_width)
    global_peak = lax.pmax(row_peak, "ka")
    factor = jnp.exp(row_peak - global_peak)
    weighted_own, mass_own = (
        lax.psum_scatter(weighted * factor[:, None], "ka", scatter_dimension=0, tiled=True),
        lax.psum_scatter(row_mass * factor, "ka", scatter_dimension=0, tiled=True),
    )
    message = (weighted_own / mass_own[:, None]).astype(jnp.bfloat16)
    mixed_rows = (
        feat_first.astype(jnp.float32)
        + jnp.dot(message, out_weight, preferred_element_type=jnp.float32)
    ).astype(jnp.bfloat16)
    strip_rows = own_rows // WIMG
    strip_image = mixed_rows.reshape(strip_rows, WIMG, feat_width)
    tile_image = lax.all_to_all(strip_image, "ka", split_axis=1, concat_axis=0, tiled=True)
    padded = padded_2(tile_image, (("pb", 0), ("ka", 1)), 1)
    result = refine(padded, tile_image, conv_weight, conv_bias)
    refined = lax.all_to_all(result, "ka", split_axis=0, concat_axis=1, tiled=True)
    return refined


def solution(mesh):
    in_specs = (P(("pb", "ka"), None), P(("ka", "pb"), None), P(), P(), P(), P())
    out_specs = P(("pb", "ka"), None, None)
    return jax.shard_map(local, mesh=mesh, in_specs=in_specs, out_specs=out_specs, check_vma=False)
```

profile of v0, /device:TPU:0, one launch (start us, length us, event | category | flops | bytes accessed | tf_op | source)
XLA Modules:
  0.0 137.4 jit_solution(6637501531085449038)
XLA Ops:
  6.5 16.9 %all_gather.9 = bf16[2048,128]{1,0:T(8,128)(2,1)S(1)} all-gather(bf16[256,128]{1,0:T(8,128)(2,1)} %param.8), channel_id=1, replica_groups=mesh['pb'=4,'ka'=8] {'ka'}, dimensions={0}, use_global_device_ids=true | all-gather | bytes 589824 | tf_op jit(solution)/shard_map/all_gather | solution.py:46
  23.5 9.3 %all_gather.10 = bf16[1024,128]{1,0:T(8,128)(2,1)S(1)} all-gather(bf16[256,128]{1,0:T(8,128)(2,1)} %param.9), channel_id=1, replica_groups=mesh['pb'=4,'ka'=8] {'pb'}, dimensions={0}, use_global_device_ids=true | all-gather | bytes 327680 | tf_op jit(solution)/shard_map/all_gather | solution.py:56
  32.7 1.0 convolution_convert_fusion
  33.7 9.0 %all_gather.11 = bf16[1024,128]{1,0:T(8,128)(2,1)S(1)} all-gather(bf16[256,128]{1,0:T(8,128)(2,1)S(1)} %convolution_convert_fusion), channel_id=1, replica_groups=mesh['pb'=4,'ka'=8] {'pb'}, dimensions={0}, use_global_device_ids=true | all-gather | bytes 327680 | tf_op jit(solution)/shard_map/all_gather | solution.py:57
  42.8 5.1 %while.14 = (s32[]{:T(128)}, f32[2,1024]{1,0:T(2,128)S(1)}, f32[2,1024]{1,0:T(2,128)S(1)}, f32[2,1024,128]{2,1,0:T(8,128)S(1)}, bf16[2,1024,128]{2,1,0:T(8,128)(...) while((s32[]{:T(128)}, f32[2,1024]{1,0:T(2,128)S(1)}, ...), condition=%wide.region_3.4_spmd, body=%wide.region_0.3_spmd.sunk | while | flops 545394688 | bytes 13955181 | solution.py:74
  43.5 0.9 fusion.79
  44.4 0.7 fusion.78
  45.3 0.7 multiply_reduce_fusion.2
  46.1 0.9 fusion.79
  47.0 0.7 fusion.78
  47.9 14.0 %pmax.7 = f32[2048]{0:T(1024)S(1)} all-reduce(f32[2048]{0:T(1024)S(1)} %bitcast.120), channel_id=1, replica_groups=mesh['pb'=4,'ka'=8] {'ka'}, use_global_device_ids=true, to_apply=%region_4.5 | all-reduce | flops 2048 | bytes 16384 | tf_op jit(solution)/shard_map/pmax | solution.py:78
  62.0 1.3 bitcast_multiply_fusion
  64.6 14.1 %all-reduce = f32[2048]{0:T(1024)S(1)} all-reduce(f32[2048]{0:T(1024)S(1)} %get-tuple-element.61), channel_id=3, replica_groups=mesh['pb'=4,'ka'=8] {'ka'}, use_global_device_ids=true, to_apply=%region_6.7.clone | all-reduce | flops 2048 | bytes 16384
  78.8 14.5 %reduce-scatter.2.cloned.1.call-done = f32[256,128]{1,0:T(8,128)} async-done(((f32[2048,128]{1,0:T(8,128)}), f32[256,128]{1,0:T(8,128)}) %reduce-scatter.2.cloned.1.call-update) | async-done | bytes 131088 | tf_op jit(solution)/shard_map/reduce_scatter | solution.py:81
  93.3 1.1 fusion.22
  95.1 1.0 reduce
  96.1 8.3 %all_to_all.24 = bf16[8,2,2048]{2,1,0:T(2,128)(2,1)S(1)} all-to-all(bf16[8,2,2048]{2,1,0:T(2,128)(2,1)S(1)} %reshape.109), channel_id=1, replica_groups=mesh['pb'=4,'ka'=8] {'ka'}, dimensions={0} | all-to-all | bytes 131072 | tf_op jit(solution)/shard_map/all_to_all | solution.py:91
  104.5 3.3 %collective-permute-start = (bf16[1,32,128]{2,1,0:T(8,128)(2,1)S(1)}, bf16[1,32,128]{2,1,0:T(8,128)(2,1)S(1)}, u32[]{:S(2)}, u32[]{:S(2)}) collective-permute-start(bf16[1,32,128]{2,1,0:T(8,128)(2,1)S(1)} %copy.17), channel_id=1, source_target_pairs={{0,8},{8,16},{16,24},{1,9},{9,17},{17,25},{2,10},{10,18},{18,26},{... | collective-permute-start | bytes 24584 | tf_op jit(solution)/shard_map/ppermute | solution.py:17
  107.9 1.3 collective-permute-start.1
  109.2 4.2 %collective-permute-done.1 = bf16[1,32,128]{2,1,0:T(8,128)(2,1)S(1)} collective-permute-done((bf16[1,32,128]{2,1,0:T(8,128)(2,1)S(1)}, bf16[1,32,128]{2,1,0:T(8,128)(2,1)S(1)}, u32[]{:S(2)}, u32[]{:S(2)}) %collective-permute-start.1) | collective-permute-done | bytes 8224 | tf_op jit(solution)/shard_map/ppermute | solution.py:20
  113.5 1.3 collective-permute-start.2
  114.8 1.3 collective-permute-start.3
  116.2 2.5 %collective-permute-done.3 = bf16[10,1,128]{2,1,0:T(2,128)(2,1)S(1)} collective-permute-done((bf16[10,1,128]{2,1,0:T(2,128)(2,1)S(1)}, bf16[10,1,128]{2,1,0:T(2,128)(2,1)S(1)}, u32[]{:S(2)}, u32[]{:S(2)}) %collective-permute-start.3) | collective-permute-done | bytes 2592 | tf_op jit(solution)/shard_map/ppermute | solution.py:20
  120.2 9.7 %all_to_all.25 = bf16[8,32,128]{2,1,0:T(8,128)(2,1)S(1)} all-to-all(bf16[8,32,128]{2,1,0:T(8,128)(2,1)S(1)} %fusion.31), channel_id=1, replica_groups=mesh['pb'=4,'ka'=8] {'ka'}, dimensions={0} | all-to-all | bytes 131072 | tf_op jit(solution)/shard_map/all_to_all | solution.py:94
  (56 shorter events, 4.6 us)
Async XLA Ops:
  6.5 26.2 %copy-start = (bf16[128,128]{1,0:T(8,128)(2,1)S(1)}, bf16[128,128]{1,0:T(8,128)(2,1)}, u32[]{:S(2)}) copy-start(bf16[128,128]{1,0:T(8,128)(2,1)} %param.10) | copy-start | bytes 98308
  6.5 86.8 %reduce-scatter.2.cloned.1.call-start = ((), (), s32[]{:S(2)}) async-start(), calls=%async_computation.3 | async-start | bytes 1179648 | tf_op jit(solution)/shard_map/reduce_scatter | solution.py:81
  42.8 20.6 %copy-start.5 = (u32[32]{0:T(128)S(1)}, u32[32]{0:T(128)}, u32[]{:S(2)}) copy-start(u32[32]{0:T(128)} %constant.42) | copy-start | bytes 388
  42.8 50.6 %copy-start.2 = (bf16[256,128]{1,0:T(8,128)(2,1)S(1)}, bf16[256,128]{1,0:T(8,128)(2,1)}, u32[]{:S(2)}) copy-start(bf16[256,128]{1,0:T(8,128)(2,1)} %param.8) | copy-start | bytes 196612
  42.8 50.5 %copy-start.3 = (bf16[128,128]{1,0:T(8,128)(2,1)S(1)}, bf16[128,128]{1,0:T(8,128)(2,1)}, u32[]{:S(2)}) copy-start(bf16[128,128]{1,0:T(8,128)(2,1)} %param.11) | copy-start | bytes 98308
  47.9 61.3 %copy-start.4 = (bf16[128]{0:T(256)(128)(2,1)S(1)}, bf16[128]{0:T(256)(128)(2,1)}, u32[]{:S(2)}) copy-start(bf16[128]{0:T(256)(128)(2,1)} %param.13) | copy-start | bytes 772
  47.9 68.2 %copy-start.1 = (bf16[3,3,128,128]{3,2,1,0:T(8,128)(2,1)S(1)}, bf16[3,3,128,128]{3,2,1,0:T(8,128)(2,1)}, u32[]{:S(2)}) copy-start(bf16[3,3,128,128]{3,2,1,0:T(8,128)(2,1)} %param.12) | copy-start | bytes 884740
  104.5 4.7 %collective-permute-start = (bf16[1,32,128]{2,1,0:T(8,128)(2,1)S(1)}, bf16[1,32,128]{2,1,0:T(8,128)(2,1)S(1)}, u32[]{:S(2)}, u32[]{:S(2)}) collective-permute-start(bf16[1,32,128]{2,1,0:T(8,128)(2,1)S(1)} %copy.17), channel_id=1, source_target_pairs={{0,8},{8,16},{16,24},{1,9},{9,17},{17,25},{2,10},{10,18},{18,26},{... | collective-permute-start | bytes 24584 | tf_op jit(solution)/shard_map/ppermute | solution.py:17
  107.9 5.5 %collective-permute-start.1 = (bf16[1,32,128]{2,1,0:T(8,128)(2,1)S(1)}, bf16[1,32,128]{2,1,0:T(8,128)(2,1)S(1)}, u32[]{:S(2)}, u32[]{:S(2)}) collective-permute-start(bf16[1,32,128]{2,1,0:T(8,128)(2,1)S(1)} %copy.18), channel_id=1, source_target_pairs={{8,0},{16,8},{24,16},{9,1},{17,9},{25,17},{10,2},{18,10},{26,18},{... | collective-permute-start | bytes 24584 | tf_op jit(solution)/shard_map/ppermute | solution.py:20
  113.5 2.8 %collective-permute-start.2 = (bf16[10,1,128]{2,1,0:T(2,128)(2,1)S(1)}, bf16[10,1,128]{2,1,0:T(2,128)(2,1)S(1)}, u32[]{:S(2)}, u32[]{:S(2)}) collective-permute-start(bf16[10,1,128]{2,1,0:T(2,128)(2,1)S(1)} %get-tuple-element.77), channel_id=1, source_target_pairs={{0,1},{1,2},{2,3},{3,4},{4,5},{5,6},{6,7},{8,9},{9,10},{10,11},{11... | collective-permute-start | bytes 7688 | tf_op jit(solution)/shard_map/ppermute | solution.py:17
  114.8 4.0 %collective-permute-start.3 = (bf16[10,1,128]{2,1,0:T(2,128)(2,1)S(1)}, bf16[10,1,128]{2,1,0:T(2,128)(2,1)S(1)}, u32[]{:S(2)}, u32[]{:S(2)}) collective-permute-start(bf16[10,1,128]{2,1,0:T(2,128)(2,1)S(1)} %get-tuple-element.78), channel_id=1, source_target_pairs={{1,0},{2,1},{3,2},{4,3},{5,4},{6,5},{7,6},{9,8},{10,9},{11,10},{12... | collective-permute-start | bytes 7688 | tf_op jit(solution)/shard_map/ppermute | solution.py:20
Sparse Core Ops, SparseCore 0:
  63.4 29.8 reduce-scatter.1
where the time goes:
time: 138 us; the launch traced here: 137 us
  blocking collectives  81.3 us (59%)
  waiting for transfers between devices  21.3 us (15%)
  between operations  14.3 us (10%)
  starting transfers between devices  7.21 us (5%)
  matrix products  6.7 us (5%)
  other arithmetic  3.99 us (3%)
  local copies, waits for them, and re-layouts  2.35 us (2%)
    all_gather x1, blocking collectives, local(): queries = lax.all_gather(feat_first, 'ka', axis=0, tiled=True)  16.9 us
    reduce_scatter x1, waiting for transfers between devices, local(): lax.psum_scatter(weighted * factor[:, None], 'ka', scatter_dimension=0, t...  14.5 us
    unnamed x1, blocking collectives  14.1 us
    pmax x1, blocking collectives, local(): global_peak = lax.pmax(row_peak, 'ka')  14 us
    all_to_all x1, blocking collectives, local(): lax.all_to_all(result, 'ka', split_axis=0, concat_axis=1, tiled=True)  9.68 us
    all_gather x1, blocking collectives, local(): keys_part = lax.all_gather(feat_second, 'pb', axis=0, tiled=True)  9.27 us
    all_gather x1, blocking collectives, local(): values_part = lax.all_gather(values, 'pb', axis=0, tiled=True)  9.04 us
    all_to_all x1, blocking collectives, local(): lax.all_to_all(strip_image, 'ka', split_axis=1, concat_axis=0, tiled=True)  8.3 us
  transfers between devices with their start and end apart: 5, of which 3 were waited for; matrix products, arithmetic and copies ran while one was open for 1% of the time, Pallas kernels for 0%

commit v1 on v0

v1 whole, which is shorter than its diff:
```python
import functools
import math

import jax
import jax.numpy as jnp
from jax import lax
from jax.experimental import pallas as pl
from jax.experimental.pallas import tpu as pltpu
from jax.sharding import PartitionSpec as P

WIMG = 256
MESH = pl.DeviceIdType.MESH


def kernel(
    n_pb, n_ka,
    q_ref, k_ref, vw_ref, ow_ref, cw_ref, cb_ref, out_ref,
    keys, peer_q, acc, peak, part_out, part_in, mixed, halo,
    z_send, xy_send, key_recv, one_send, one_recv,
):
    rows, width = q_ref.shape
    n_z = n_ka // 2
    bits = [1 << b for b in range(n_pb.bit_length() - 1)]
    orders = (bits, bits[::-1])
    half = rows // 2
    scale = math.log2(math.e) * width ** -0.5

    pb, ka = lax.axis_index("pb"), lax.axis_index("ka")
    z, core = ka // 2, ka % 2
    partner = (pb, z * 2 + 1 - core)
    line = [(pb, lax.rem(z + n_z - k, n_z) * 2 + core) for k in range(1, n_z)]
    across = {b: (pb + b - 2 * b * (pb // b % 2), ka) for b in bits}
    n_rows = n_pb * n_ka
    row = pb * n_ka + ka
    above, below = lax.rem(row + n_rows - 1, n_rows), lax.rem(row + 1, n_rows)
    above_id, below_id = (above // n_ka, above % n_ka), (below // n_ka, below % n_ka)

    barrier = pltpu.get_barrier_semaphore()
    greeted = [partner, above_id, below_id] + line + list(across.values())
    for device in greeted:
        pl.semaphore_signal(barrier, inc=1, device_id=device, device_id_type=MESH)
    keys[0, 0] = k_ref[...]
    pl.semaphore_wait(barrier, len(greeted))

    started = []

    def send(src, dst, send_sem, recv_sem, device):
        copy = pltpu.make_async_remote_copy(
            src_ref=src, dst_ref=dst, send_sem=send_sem, recv_sem=recv_sem,
            device_id=device, device_id_type=MESH,
        )
        copy.start()
        started.append(copy)
        return copy

    def piece(j, k, f):
        return keys.at[j, k, pl.ds(f * half, half)]

    def hop(j, k, f, bit):
        send(
            piece(j, k, f), piece(j ^ bit, k, f),
            xy_send.at[j ^ bit, k, f], key_recv.at[j ^ bit, k, f], across[bit],
        )

    def arrived(j, k, f):
        ref = piece(j, k, f)
        pltpu.make_async_copy(ref, ref, key_recv.at[j, k, f]).wait()

    def forward(j, k, f):
        last = max([i for i, b in enumerate(orders[f]) if j & b], default=-1)
        for bit in orders[f][last + 1:]:
            hop(j, k, f, bit)

    q_copy = send(q_ref, peer_q, one_send.at[0], one_recv.at[0], partner)
    for f in range(2):
        forward(0, 0, f)
        for k in range(1, n_z):
            send(
                piece(0, 0, f), piece(0, k, f),
                z_send.at[k, f], key_recv.at[0, k, f], line[k - 1],
            )

    def attend(j, side, first):
        queries = (peer_q if side == 0 else q_ref)[...]
        block = keys[j].reshape(n_z * rows, width)
        scores = lax.dot_general(
            queries, block, (((1,), (1,)), ((), ())), preferred_element_type=jnp.float32
        ) * scale
        top = jnp.max(scores, axis=1, keepdims=True)
        if not first:
            top = jnp.maximum(top, peak[side][:, :1])
        weights = jnp.exp2(scores - top).astype(jnp.bfloat16)
        extended = jnp.concatenate([block, jnp.ones_like(block)], axis=1)
        total = jnp.dot(weights, extended, preferred_element_type=jnp.float32)
        if not first:
            total = total + acc[side] * jnp.exp2(peak[side][:, :1] - top)
        acc[side] = total
        peak[side] = jnp.broadcast_to(top, (rows, width))

    def receive(j, k):
        for f in range(2):
            arrived(j, k, f)
            forward(j, k, f)

    for k in range(1, n_z):
        receive(0, k)
    q_copy.wait_recv()
    for j in range(n_pb):
        if j:
            for k in range(n_z):
                receive(j, k)
        attend(j, 0, j == 0)
        if j == n_pb - 1:
            lane = lax.broadcasted_iota(jnp.int32, (rows, width), 1)
            part_out[:, :width] = acc[0, :, :width]
            part_out[:, width:] = jnp.where(lane < width // 2, acc[0, :, width:], peak[0])
            part_copy = send(part_out, part_in, one_send.at[1], one_recv.at[1], partner)
        attend(j, 1, j == 0)

    part_copy.wait_recv()
    other_peak = part_in[:, width + width // 2:width + width // 2 + 1]
    other_mass = part_in[:, width:width + 1]
    own_peak = peak[1][:, :1]
    top = jnp.maximum(own_peak, other_peak)
    own_factor, other_factor = jnp.exp2(own_peak - top), jnp.exp2(other_peak - top)
    mass = acc[1, :, width:width + 1] * own_factor + other_mass * other_factor
    blend = (acc[1, :, :width] * own_factor + part_in[:, :width] * other_factor) / mass
    message = jnp.dot(
        blend.astype(jnp.bfloat16), vw_ref[...], preferred_element_type=jnp.float32
    ).astype(jnp.bfloat16)
    mixed[...] = (
        q_ref[...].astype(jnp.float32)
        + jnp.dot(message, ow_ref[...], preferred_element_type=jnp.float32)
    ).astype(jnp.bfloat16)
    down = send(mixed, halo.at[0], one_send.at[2], one_recv.at[2], below_id)
    up = send(mixed, halo.at[1], one_send.at[3], one_recv.at[3], above_id)

    def taps(image, a):
        return [
            jnp.dot(image, cw_ref[a, b], preferred_element_type=jnp.float32) for b in range(3)
        ]

    own = taps(mixed[...], 1)
    down.wait_recv()
    up.wait_recv()
    upper = jnp.where(row > 0, halo[0], jnp.zeros_like(halo[0]))
    lower = jnp.where(row < n_rows - 1, halo[1], jnp.zeros_like(halo[1]))
    left, centre, right = [
        x + y + w for x, y, w in zip(own, taps(upper, 0), taps(lower, 2))
    ]
    column = lax.broadcasted_iota(jnp.int32, (rows, width), 0)
    conv = (
        centre
        + jnp.where(column > 0, pltpu.roll(left, 1, 0), 0.0)
        + jnp.where(column < rows - 1, pltpu.roll(right, rows - 1, 0), 0.0)
        + cb_ref[...].astype(jnp.float32)
    )
    out_ref[...] = (mixed[...].astype(jnp.float32) + jax.nn.gelu(conv)).astype(jnp.bfloat16)
    for copy in started:
        copy.wait_send()


def solution(mesh):
    n_pb, n_ka = mesh.shape["pb"], mesh.shape["ka"]

    def local(feat_first, feat_second, value_weight, out_weight, conv_weight, conv_bias):
        rows, width = feat_first.shape
        assert rows == WIMG and n_ka % 2 == 0 and n_pb & (n_pb - 1) == 0
        n_z = n_ka // 2
        vmem = pl.BlockSpec(memory_space=pltpu.VMEM)
        dma = pltpu.SemaphoreType.DMA
        out = pl.pallas_call(
            functools.partial(kernel, n_pb, n_ka),
            out_shape=jax.ShapeDtypeStruct((rows, width), jnp.bfloat16),
            in_specs=[vmem] * 6,
            out_specs=vmem,
            scratch_shapes=[
                pltpu.VMEM((n_pb, n_z, rows, width), jnp.bfloat16),
                pltpu.VMEM((rows, width), jnp.bfloat16),
                pltpu.VMEM((2, rows, 2 * width), jnp.float32),
                pltpu.VMEM((2, rows, width), jnp.float32),
                pltpu.VMEM((rows, 2 * width), jnp.float32),
                pltpu.VMEM((rows, 2 * width), jnp.float32),
                pltpu.VMEM((rows, width), jnp.bfloat16),
                pltpu.VMEM((2, rows, width), jnp.bfloat16),
                dma((n_z, 2)),
                dma((n_pb, n_z, 2)),
                dma((n_pb, n_z, 2)),
                dma((4,)),
                dma((4,)),
            ],
            compiler_params=pltpu.CompilerParams(
                collective_id=0, has_side_effects=True, vmem_limit_bytes=48 * 1024 * 1024
            ),
        )(feat_first, feat_second, value_weight, out_weight, conv_weight, conv_bias.reshape(1, width))
        return out.reshape(rows // WIMG, WIMG, width)

    in_specs = (P(("pb", "ka"), None), P(("ka", "pb"), None), P(), P(), P(), P())
    out_specs = P(("pb", "ka"), None, None)
    return jax.shard_map(local, mesh=mesh, in_specs=in_specs, out_specs=out_specs, check_vma=False)
```

time: 138 us -> 37 us (0.27)
  blocking collectives: 81.3 us -> 0 us
  Pallas kernels: 0 us -> 31.2 us
  waiting for transfers between devices: 21.3 us -> 0 us
  between operations: 14.3 us -> 0.02 us
  starting transfers between devices: 7.21 us -> 0 us
  matrix products: 6.7 us -> 0 us
  other arithmetic: 3.99 us -> 0 us
  local copies, waits for them, and re-layouts: 2.35 us -> 5.44 us
    all_gather x3 -> x0, blocking collectives: 35.2 us -> none  [the longest x1 16.9 us: local(): queries = lax.all_gather(feat_first, 'ka', axis=0, tiled=True)]
    pallas_call x0 -> x1, Pallas kernels: none -> 31.2 us  [local(): pl.pallas_call(functools.partial(kernel, n_pb, n_ka), out_shape=jax.Shape...]
    all_to_all x2 -> x0, blocking collectives: 18 us -> none  [the longest x1 9.68 us: local(): lax.all_to_all(result, 'ka', split_axis=0, concat_axis=1, tiled=True)]
    reduce_scatter x1 -> x0, waiting for transfers between devices: 14.5 us -> none  [local(): lax.psum_scatter(weighted * factor[:, None], 'ka', scatter_dimension=0, t...]
    unnamed x1 -> x0, blocking collectives: 14.1 us -> none
    pmax x1 -> x0, blocking collectives: 14 us -> none  [local(): global_peak = lax.pmax(row_peak, 'ka')]
    ppermute x4 -> x0, starting transfers between devices: 7.21 us -> none  [the longest x2 4.63 us: padded_2(): lax.ppermute(lax.slice_in_dim(block, block.shape[dim] - width, None, axis...]
    ppermute x4 -> x0, waiting for transfers between devices: 6.75 us -> none  [the longest x2 6.74 us: padded_2(): lax.ppermute(lax.slice_in_dim(block, 0, width, axis=dim), axis, backward)]
  transfers between devices with their start and end apart: 5 -> 0, of which waited for: 3 -> 0; matrix products, arithmetic and copies ran while one was open for 1% -> 0% of each run, Pallas kernels for 0% -> 0%
where the time goes in v1:
time: 37 us; the launch traced here: 36.6 us
  Pallas kernels  31.2 us (84%)
  local copies, waits for them, and re-layouts  5.44 us (15%)
    pallas_call x1, Pallas kernels, local(): pl.pallas_call(functools.partial(kernel, n_pb, n_ka), out_shape=jax.Shape...  31.2 us
    unnamed x13, local copies, waits for them, and re-layouts  5.44 us

profile of v1, /device:TPU:0, one launch (start us, length us, event | category | flops | bytes accessed | tf_op | source)
XLA Modules:
  0.0 36.6 jit_solution(17486507083590322162)
XLA Ops:
  0.0 0.0 copy-start.5
  0.0 0.7 %copy-done.5 = bf16[128]{0:T(256)(128)(2,1)S(1)} copy-done((bf16[128]{0:T(256)(128)(2,1)S(1)}, bf16[128]{0:T(256)(128)(2,1)}, u32[]{:S(2)}) %copy-start.5) | copy-done | bytes 280
  0.7 0.0 copy-start
  0.7 1.0 %copy-done = bf16[3,3,128,128]{3,2,1,0:T(8,128)(2,1)S(1)} copy-done((bf16[3,3,128,128]{3,2,1,0:T(8,128)(2,1)S(1)}, bf16[3,3,128,128]{3,2,1,0:T(8,128)(2,1)}, u32[]{:S(2)}) %copy-start) | copy-done | bytes 294936
  1.6 0.0 copy-start.1
  1.6 0.8 %copy-done.1 = bf16[256,128]{1,0:T(8,128)(2,1)S(1)} copy-done((bf16[256,128]{1,0:T(8,128)(2,1)S(1)}, bf16[256,128]{1,0:T(8,128)(2,1)}, u32[]{:S(2)}) %copy-start.1) | copy-done | bytes 65560
  2.5 0.0 copy-start.2
  2.5 0.8 %copy-done.2 = bf16[256,128]{1,0:T(8,128)(2,1)S(1)} copy-done((bf16[256,128]{1,0:T(8,128)(2,1)S(1)}, bf16[256,128]{1,0:T(8,128)(2,1)}, u32[]{:S(2)}) %copy-start.2) | copy-done | bytes 65560
  3.3 0.0 copy-start.3
  3.3 0.8 %copy-done.3 = bf16[128,128]{1,0:T(8,128)(2,1)S(1)} copy-done((bf16[128,128]{1,0:T(8,128)(2,1)S(1)}, bf16[128,128]{1,0:T(8,128)(2,1)}, u32[]{:S(2)}) %copy-start.3) | copy-done | bytes 32792
  4.1 0.0 copy-start.4
  4.1 0.8 %copy-done.4 = bf16[128,128]{1,0:T(8,128)(2,1)S(1)} copy-done((bf16[128,128]{1,0:T(8,128)(2,1)S(1)}, bf16[128,128]{1,0:T(8,128)(2,1)}, u32[]{:S(2)}) %copy-start.4) | copy-done | bytes 32792
  4.8 31.2 %shard_map.64 = bf16[256,128]{1,0:T(8,128)(2,1)S(1)} custom-call(bf16[256,128]{1,0:T(8,128)(2,1)S(1)} %copy-done.1, bf16[256,128]{1,0:T(8,128)(2,1)S(1)} %copy-done.2, bf16[128,128]{1,0:T(8,128)(2,1)S(1)} %copy-done.3, bf16[128,128]{1,0:T(8,128)(2,1)S(1)} %copy-done.4, bf16[3,3,128,128]{3,2,1,0:T(8,128)(2,1)S(1)} %copy-done, bf16[1,128]{1,0:T(2,128)(2,1)S(1)} %bitcast.3), custom_call_target="tpu_custom_call" | custom-call | tf_op jit(solution)/shard_map/pallas_call | solution.py:172
  36.0 0.6 %copy.8 = bf16[1,256,128]{2,1,0:T(8,128)(2,1)} copy(bf16[1,256,128]{2,1,0:T(8,128)(2,1)S(1)} %bitcast.2) | data formatting | bytes 131072
Async XLA Ops:
  0.0 0.7 %copy-start.5 = (bf16[128]{0:T(256)(128)(2,1)S(1)}, bf16[128]{0:T(256)(128)(2,1)}, u32[]{:S(2)}) copy-start(bf16[128]{0:T(256)(128)(2,1)} %param.11) | copy-start | bytes 772
  0.7 1.0 %copy-start = (bf16[3,3,128,128]{3,2,1,0:T(8,128)(2,1)S(1)}, bf16[3,3,128,128]{3,2,1,0:T(8,128)(2,1)}, u32[]{:S(2)}) copy-start(bf16[3,3,128,128]{3,2,1,0:T(8,128)(2,1)} %cw_ref.1) | copy-start | bytes 884740
  1.6 0.8 %copy-start.1 = (bf16[256,128]{1,0:T(8,128)(2,1)S(1)}, bf16[256,128]{1,0:T(8,128)(2,1)}, u32[]{:S(2)}) copy-start(bf16[256,128]{1,0:T(8,128)(2,1)} %q_ref.1) | copy-start | bytes 196612
  2.5 0.8 %copy-start.2 = (bf16[256,128]{1,0:T(8,128)(2,1)S(1)}, bf16[256,128]{1,0:T(8,128)(2,1)}, u32[]{:S(2)}) copy-start(bf16[256,128]{1,0:T(8,128)(2,1)} %k_ref.1) | copy-start | bytes 196612
  3.3 0.8 %copy-start.3 = (bf16[128,128]{1,0:T(8,128)(2,1)S(1)}, bf16[128,128]{1,0:T(8,128)(2,1)}, u32[]{:S(2)}) copy-start(bf16[128,128]{1,0:T(8,128)(2,1)} %vw_ref.1) | copy-start | bytes 98308
  4.1 0.8 %copy-start.4 = (bf16[128,128]{1,0:T(8,128)(2,1)S(1)}, bf16[128,128]{1,0:T(8,128)(2,1)}, u32[]{:S(2)}) copy-start(bf16[128,128]{1,0:T(8,128)(2,1)} %ow_ref.1) | copy-start | bytes 98308

commit v2 on v1

--- a/solution.py
+++ b/solution.py
@@ -14,9 +14,10 @@
 
 def kernel(
     n_pb, n_ka,
-    q_ref, k_ref, vw_ref, ow_ref, cw_ref, cb_ref, out_ref,
+    q_hbm, k_hbm, vw_hbm, ow_hbm, cw_hbm, cb_hbm, out_ref,
+    q_ref, vw_ref, ow_ref, cw_ref, cb_ref,
     keys, peer_q, acc, peak, part_out, part_in, mixed, halo,
-    z_send, xy_send, key_recv, one_send, one_recv,
+    local_sem, z_send, xy_send, key_recv, one_send, one_recv,
 ):
     rows, width = q_ref.shape
     n_z = n_ka // 2
@@ -39,7 +40,15 @@
     greeted = [partner, above_id, below_id] + line + list(across.values())
     for device in greeted:
         pl.semaphore_signal(barrier, inc=1, device_id=device, device_id_type=MESH)
-    keys[0, 0] = k_ref[...]
+    fetches = [
+        pltpu.make_async_copy(src, dst, local_sem.at[i])
+        for i, (src, dst) in enumerate((
+            (k_hbm, keys.at[0, 0]), (q_hbm, q_ref), (vw_hbm, vw_ref),
+            (ow_hbm, ow_ref), (cw_hbm, cw_ref), (cb_hbm, cb_ref),
+        ))
+    ]
+    for fetch in fetches:
+        fetch.start()
     pl.semaphore_wait(barrier, len(greeted))
 
     started = []
@@ -56,9 +65,12 @@
     def piece(j, k, f):
         return keys.at[j, k, pl.ds(f * half, half)]
 
+    def source(j, k, f):
+        return piece(j, k, f) if j or k else k_hbm.at[pl.ds(f * half, half)]
+
     def hop(j, k, f, bit):
         send(
-            piece(j, k, f), piece(j ^ bit, k, f),
+            source(j, k, f), piece(j ^ bit, k, f),
             xy_send.at[j ^ bit, k, f], key_recv.at[j ^ bit, k, f], across[bit],
         )
 
@@ -66,25 +78,26 @@
         ref = piece(j, k, f)
         pltpu.make_async_copy(ref, ref, key_recv.at[j, k, f]).wait()
 
+    def onward(j, f):
+        last = max([i for i, b in enumerate(orders[f]) if j & b], default=-1)
+        return orders[f][last + 1:]
+
     def forward(j, k, f):
-        last = max([i for i, b in enumerate(orders[f]) if j & b], default=-1)
-        for bit in orders[f][last + 1:]:
+        for bit in onward(j, f):
             hop(j, k, f, bit)
 
-    q_copy = send(q_ref, peer_q, one_send.at[0], one_recv.at[0], partner)
-    for f in range(2):
-        forward(0, 0, f)
-        for k in range(1, n_z):
-            send(
-                piece(0, 0, f), piece(0, k, f),
-                z_send.at[k, f], key_recv.at[0, k, f], line[k - 1],
-            )
-
-    def attend(j, side, first):
-        queries = (peer_q if side == 0 else q_ref)[...]
-        block = keys[j].reshape(n_z * rows, width)
+    def receive(j, k, f):
+        arrived(j, k, f)
+        forward(j, k, f)
+
+    def queries_of(side):
+        return peer_q if side == 0 else q_ref
+
+    def attend(j, k0, k1, side, first=False):
+        block = keys[j, k0:k1].reshape((k1 - k0) * rows, width)
         scores = lax.dot_general(
-            queries, block, (((1,), (1,)), ((), ())), preferred_element_type=jnp.float32
+            queries_of(side)[...], block, (((1,), (1,)), ((), ())),
+            preferred_element_type=jnp.float32,
         ) * scale
         top = jnp.max(scores, axis=1, keepdims=True)
         if not first:
@@ -97,26 +110,57 @@
         acc[side] = total
         peak[side] = jnp.broadcast_to(top, (rows, width))
 
-    def receive(j, k):
+    for f in range(2):
+        forward(0, 0, f)
+        for k in range(1, n_z):
+            send(
+                source(0, 0, f), piece(0, k, f),
+                z_send.at[k, f], key_recv.at[0, k, f], line[k - 1],
+            )
+    q_copy = send(q_hbm, peer_q, one_send.at[0], one_recv.at[0], partner)
+    fetches[0].wait()
+    fetches[1].wait()
+
+    relayed = sorted(
+        (bin(j).count("1"), j, f)
+        for f in range(2) for j in range(1, n_pb) if onward(j, f)
+    )
+    halfway = (n_z + 1) // 2
+
+    def relay(k):
+        for _, j, f in relayed:
+            receive(j, k, f)
+
+    for k in range(1, n_z):
         for f in range(2):
-            arrived(j, k, f)
-            forward(j, k, f)
-
-    for k in range(1, n_z):
-        receive(0, k)
-    q_copy.wait_recv()
-    for j in range(n_pb):
-        if j:
-            for k in range(n_z):
-                receive(j, k)
-        attend(j, 0, j == 0)
-        if j == n_pb - 1:
-            lane = lax.broadcasted_iota(jnp.int32, (rows, width), 1)
-            part_out[:, :width] = acc[0, :, :width]
-            part_out[:, width:] = jnp.where(lane < width // 2, acc[0, :, width:], peak[0])
-            part_copy = send(part_out, part_in, one_send.at[1], one_recv.at[1], partner)
-        attend(j, 1, j == 0)
-
+            receive(0, k, f)
+        relay(k - 1)
+        if k == 1:
+            q_copy.wait_recv()
+        if k == halfway:
+            for side in range(2):
+                attend(0, 0, halfway, side, first=True)
+    relay(n_z - 1)
+    for side in range(2):
+        attend(0, halfway, n_z, side)
+    for j in range(1, n_pb):
+        last = j == n_pb - 1
+        parts = ((0, halfway), (halfway, n_z)) if last else ((0, n_z),)
+        for k0, k1 in parts:
+            for k in range(k0, k1):
+                for f in range(2):
+                    if not onward(j, f):
+                        arrived(j, k, f)
+            attend(j, k0, k1, 0)
+            if last and k1 == n_z:
+                lane = lax.broadcasted_iota(jnp.int32, (rows, width), 1)
+                part_out[:, :width] = acc[0, :, :width]
+                part_out[:, width:] = jnp.where(lane < width // 2, acc[0, :, width:], peak[0])
+                part_copy = send(part_out, part_in, one_send.at[1], one_recv.at[1], partner)
+            attend(j, k0, k1, 1)
+
+    for fetch in fetches[2:]:
+        fetch.wait()
     part_copy.wait_recv()
     other_peak = part_in[:, width + width // 2:width + width // 2 + 1]
     other_mass = part_in[:, width:width + 1]
@@ -172,9 +216,14 @@
         out = pl.pallas_call(
             functools.partial(kernel, n_pb, n_ka),
             out_shape=jax.ShapeDtypeStruct((rows, width), jnp.bfloat16),
-            in_specs=[vmem] * 6,
+            in_specs=[pl.BlockSpec(memory_space=pl.ANY)] * 6,
             out_specs=vmem,
             scratch_shapes=[
+                pltpu.VMEM((rows, width), jnp.bfloat16),
+                pltpu.VMEM(value_weight.shape, jnp.bfloat16),
+                pltpu.VMEM(out_weight.shape, jnp.bfloat16),
+                pltpu.VMEM(conv_weight.shape, jnp.bfloat16),
+                pltpu.VMEM((1, width), jnp.bfloat16),
                 pltpu.VMEM((n_pb, n_z, rows, width), jnp.bfloat16),
                 pltpu.VMEM((rows, width), jnp.bfloat16),
                 pltpu.VMEM((2, rows, 2 * width), jnp.float32),
@@ -183,6 +232,7 @@
                 pltpu.VMEM((rows, 2 * width), jnp.float32),
                 pltpu.VMEM((rows, width), jnp.bfloat16),
                 pltpu.VMEM((2, rows, width), jnp.bfloat16),
+                dma((6,)),
                 dma((n_z, 2)),
                 dma((n_pb, n_z, 2)),
                 dma((n_pb, n_z, 2)),
@@ -190,7 +240,7 @@
                 dma((4,)),
             ],
             compiler_params=pltpu.CompilerParams(
-                collective_id=0, has_side_effects=True, vmem_limit_bytes=48 * 1024 * 1024
+                collective_id=0, has_side_effects=True, vmem_limit_bytes=60 * 1024 * 1024
             ),
         )(feat_first, feat_second, value_weight, out_weight, conv_weight, conv_bias.reshape(1, width))
         return out.reshape(rows // WIMG, WIMG, width)

time: 37 us -> 35.2 us (0.951)
  local copies, waits for them, and re-layouts: 5.44 us -> 1.47 us
  Pallas kernels: 31.2 us -> 33.5 us
    unnamed x13 -> x1, local copies, waits for them, and re-layouts: 5.44 us -> 1.47 us
    pallas_call x1, Pallas kernels: 31.2 us -> 33.5 us  [local(): pl.pallas_call(functools.partial(kernel, n_pb, n_ka), out_shape=jax.Shape...]
where the time goes in v2:
time: 35.2 us; the launch traced here: 35 us
  Pallas kernels  33.5 us (95%)
  local copies, waits for them, and re-layouts  1.47 us (4%)
    pallas_call x1, Pallas kernels, local(): pl.pallas_call(functools.partial(kernel, n_pb, n_ka), out_shape=jax.Shape...  33.5 us
    unnamed x1, local copies, waits for them, and re-layouts  1.47 us

profile of v2, /device:TPU:0, one launch (start us, length us, event | category | flops | bytes accessed | tf_op | source)
XLA Modules:
  0.0 35.0 jit_solution(11430487510385036471)
XLA Ops:
  0.0 33.5 %shard_map.64 = bf16[256,128]{1,0:T(8,128)(2,1)} custom-call(bf16[256,128]{1,0:T(8,128)(2,1)} %q_hbm.1, bf16[256,128]{1,0:T(8,128)(2,1)} %k_hbm.1, bf16[128,128]{1,0:T(8,128)(2,1)} %vw_hbm.1, bf16[128,128]{1,0:T(8,128)(2,1)} %ow_hbm.1, bf16[3,3,128,128]{3,2,1,0:T(8,128)(2,1)} %cw_hbm.1, bf16[1,128]{1,0:T(2,128)(2,1)} %bitcast.3), custom_call_target="tpu_custom_call" | custom-call | tf_op jit(solution)/shard_map/pallas_call | solution.py:216
  33.5 1.5 %copy.8 = bf16[1,256,128]{2,1,0:T(8,128)(2,1)} copy(bf16[1,256,128]{2,1,0:T(8,128)(2,1)} %bitcast.2) | data formatting | bytes 131072

commit v3 on v2

--- a/solution.py
+++ b/solution.py
@@ -29,7 +29,10 @@
     pb, ka = lax.axis_index("pb"), lax.axis_index("ka")
     z, core = ka // 2, ka % 2
     partner = (pb, z * 2 + 1 - core)
-    line = [(pb, lax.rem(z + n_z - k, n_z) * 2 + core) for k in range(1, n_z)]
+    line = [(pb, lax.rem(z + n_z + step, n_z) * 2 + core) for step in (-1, 1)]
+    nearest = [
+        sorted(range(n_z), key=lambda other: (abs(other - i), i - other)) for i in range(n_z)
+    ]
     across = {b: (pb + b - 2 * b * (pb // b % 2), ka) for b in bits}
     n_rows = n_pb * n_ka
     row = pb * n_ka + ka
@@ -110,13 +113,42 @@
         acc[side] = total
         peak[side] = jnp.broadcast_to(top, (rows, width))
 
+    def z_copy(k, f, here, there, sem):
+        return pltpu.make_async_remote_copy(
+            src_ref=source(0, k, f),
+            dst_ref=piece(0, nearest[there].index(nearest[here][k]), f),
+            send_sem=z_send.at[sem, f],
+            recv_sem=key_recv.at[0, nearest[there].index(nearest[here][k]), f],
+            device_id=(pb, there * 2 + core),
+            device_id_type=MESH,
+        )
+
+    def z_hops(k, here):
+        owner = nearest[here][k]
+        return [
+            (k if there < here else n_z + k, there)
+            for there in (here - 1, here + 1)
+            if 0 <= there < n_z and (owner - here) * (there - here) <= 0
+        ]
+
+    def each_place(act):
+        for here in range(n_z):
+            pl.when(z == here)(functools.partial(act, here))
+
+    def z_forward(k, here):
+        for sem, there in z_hops(k, here):
+            for f in range(2):
+                z_copy(k, f, here, there, sem).start()
+
+    def z_drain(here):
+        for k in range(n_z):
+            for sem, there in z_hops(k, here):
+                for f in range(2):
+                    z_copy(k, f, here, there, sem).wait_send()
+
+    each_place(functools.partial(z_forward, 0))
     for f in range(2):
         forward(0, 0, f)
-        for k in range(1, n_z):
-            send(
-                source(0, 0, f), piece(0, k, f),
-                z_send.at[k, f], key_recv.at[0, k, f], line[k - 1],
-            )
     q_copy = send(q_hbm, peer_q, one_send.at[0], one_recv.at[0], partner)
     fetches[0].wait()
     fetches[1].wait()
@@ -133,7 +165,10 @@
 
     for k in range(1, n_z):
         for f in range(2):
-            receive(0, k, f)
+            arrived(0, k, f)
+        each_place(functools.partial(z_forward, k))
+        for f in range(2):
+            forward(0, k, f)
         relay(k - 1)
         if k == 1:
             q_copy.wait_recv()
@@ -202,6 +237,7 @@
     out_ref[...] = (mixed[...].astype(jnp.float32) + jax.nn.gelu(conv)).astype(jnp.bfloat16)
     for copy in started:
         copy.wait_send()
+    each_place(z_drain)
 
 
 def solution(mesh):
@@ -233,7 +269,7 @@
                 pltpu.VMEM((rows, width), jnp.bfloat16),
                 pltpu.VMEM((2, rows, width), jnp.bfloat16),
                 dma((6,)),
-                dma((n_z, 2)),
+                dma((2 * n_z, 2)),
                 dma((n_pb, n_z, 2)),
                 dma((n_pb, n_z, 2)),
                 dma((4,)),

time: 35.2 us -> 35 us (level)
  no operation moved by 1% of the time
where the time goes in v3:
time: 35 us; the launch traced here: 34.8 us
  Pallas kernels  33.4 us (95%)
  local copies, waits for them, and re-layouts  1.47 us (4%)
    pallas_call x1, Pallas kernels, local(): pl.pallas_call(functools.partial(kernel, n_pb, n_ka), out_shape=jax.Shape...  33.4 us
    unnamed x1, local copies, waits for them, and re-layouts  1.47 us

profile of v3, /device:TPU:0, one launch (start us, length us, event | category | flops | bytes accessed | tf_op | source)
XLA Modules:
  0.0 34.8 jit_solution(1592229089631490702)
XLA Ops:
  0.0 33.4 %shard_map.64 = bf16[256,128]{1,0:T(8,128)(2,1)} custom-call(bf16[256,128]{1,0:T(8,128)(2,1)} %q_hbm.1, bf16[256,128]{1,0:T(8,128)(2,1)} %k_hbm.1, bf16[128,128]{1,0:T(8,128)(2,1)} %vw_hbm.1, bf16[128,128]{1,0:T(8,128)(2,1)} %ow_hbm.1, bf16[3,3,128,128]{3,2,1,0:T(8,128)(2,1)} %cw_hbm.1, bf16[1,128]{1,0:T(2,128)(2,1)} %bitcast.3), custom_call_target="tpu_custom_call" | custom-call | tf_op jit(solution)/shard_map/pallas_call | solution.py:252
  33.4 1.5 %copy.8 = bf16[1,256,128]{2,1,0:T(8,128)(2,1)} copy(bf16[1,256,128]{2,1,0:T(8,128)(2,1)} %bitcast.2) | data formatting | bytes 131072
